TPU v7x, 256 devices: a whole 4x4x8 slice. The times are simulated.
256 devices in a mesh: section: 8 (over y, core), height: 32 (over z, x).
Axes of the slice: x: 4, y: 4, z: 8, core: 2. Of those that a mesh axis runs over, the one named last changes fastest.
Arguments:
- acts: bfloat16 [16, 1024, 2560], P(None, 'height'), may hold values from -7 to 7
- stale: bfloat16 [8, 16, 1024, 5120], P('section', None, 'height'), may hold values from -6 to 6
- layer_ids: int32 [8], P('section'), may hold values from 0 to 7, each once
- layer_gains: bfloat16 [8, 7680], replicated, may hold values from 0.25 to 4.5
- tile_lists: int32 [16, 32, 12], P(None, 'height'), may hold values from 0 to 47, as said below
- tile_counts: int32 [16, 32], P(None, 'height'), may hold values from 1 to 12, as said below
Outputs:
- latent_out: bfloat16 [16, 1024, 2560], P('section', 'height')
- kv_cache: bfloat16 [8, 16, 1024, 5120], P('section', None, 'height')
Inputs may be any that keep to these rules, and one draw needn't show every extreme that they name: `tile_lists`: entry c names the key tile of patch c // 3 at tile height h + c % 3 - 1. The first tile_counts[p, h] entries are distinct, lie inside the grid, lie within 2 patches of p, and begin with the query tile itself, 3 p + 1. Entries after the count are other candidate numbers and are ignored. `tile_counts`: some query tile has all 12 entries live.
All inputs are finite; a program needn't handle non-finite values.
Results may differ from a plain program's by a relative error of at most 0.012.
Values may be sent and summed in bfloat16 or wider, within the bound.
No kernel may reach another device: no remote copies, remote signals or barrier semaphores. Data moves between devices by JAX's collectives and lax.ppermute only.
A program may use at most 128 MiB of HBM per device.

v0:
```python
import math

import jax
import jax.numpy as jnp
from jax import lax
from jax.sharding import PartitionSpec as P

HEAD_DIM = 128
LIST = 12


def extended(block, sides, width):
    for axis, dim in sides:
        count = lax.axis_size(axis)
        forward = [(i, i + 1) for i in range(count - 1)]
        backward = [(target, source) for source, target in forward]
        low = lax.ppermute(
            lax.slice_in_dim(block, block.shape[dim] - width, None, axis=dim), axis, forward
        )
        high = lax.ppermute(lax.slice_in_dim(block, 0, width, axis=dim), axis, backward)
        block = jnp.concatenate([low, block, high], axis=dim)
    return block


def passed_along(value, axis, steps):
    count = lax.axis_size(axis)
    first, last = (max(0, -steps), min(count, count - steps))
    return lax.ppermute(value, axis, [(source, source + steps) for source in range(first, last)])


def normalize(rows):
    widened = rows.astype(jnp.float32)
    return widened / jnp.sqrt(jnp.mean(widened * widened, axis=-1, keepdims=True) + 1e-06)


def make_pairs(rows_in, gain_key, gain_value):
    normed = normalize(rows_in)
    return jnp.concatenate([normed * gain_key, normed * gain_value], axis=-1).astype(jnp.bfloat16)


def attend(current, candidates, listing, live_count, gain_query):
    tile_rows, channels = current.shape
    head_count = channels // HEAD_DIM
    queries = (
        (normalize(current) * gain_query)
        .astype(jnp.bfloat16)
        .reshape(tile_rows, head_count, HEAD_DIM)
    )
    flattened = candidates.reshape(-1, tile_rows, 2 * channels)
    picked = jnp.take(flattened, listing, axis=0).reshape(LIST * tile_rows, 2, head_count, HEAD_DIM)
    scores = jnp.einsum(
        "qhd,khd->hqk", queries, picked[:, 0], preferred_element_type=jnp.float32
    ) * (1.0 / math.sqrt(HEAD_DIM))
    living = jnp.repeat(jnp.arange(LIST, dtype=jnp.int32) < live_count, tile_rows)
    scores = jnp.where(living[None, None, :], scores, -1e30)
    highest = jnp.max(scores, axis=-1, keepdims=True)
    exponent = jnp.exp(scores - highest)
    weights = (exponent / jnp.sum(exponent, axis=-1, keepdims=True)).astype(jnp.bfloat16)
    attended = jnp.einsum("hqk,khd->qhd", weights, picked[:, 1], preferred_element_type=jnp.float32)
    return (current.astype(jnp.float32) + attended.reshape(tile_rows, channels)).astype(
        jnp.bfloat16
    )


def body(acts, stale, layer_ids, layer_gains, tile_lists, tile_counts):
    section_count = lax.axis_size("section")
    position = lax.axis_index("section")
    patch_count, tile_rows, channels = acts.shape
    selector = (jnp.arange(layer_gains.shape[0], dtype=jnp.int32) == layer_ids[0]).astype(
        jnp.bfloat16
    )
    gain_row = jnp.dot(selector, layer_gains, preferred_element_type=jnp.float32)
    gain_query = gain_row[:channels]
    gain_key = gain_row[channels : 2 * channels]
    gain_value = gain_row[2 * channels :]
    candidates = extended(stale[0], (("height", 1),), tile_rows)
    listings = tile_lists[:, 0, :]
    live_counts = tile_counts[:, 0]
    collected = jnp.zeros((patch_count, tile_rows, channels), jnp.bfloat16)
    incoming = jnp.zeros((tile_rows, channels), jnp.bfloat16)

    def advance(moment, carried):
        arriving, held, gathered_out = carried
        patch_now = moment - position
        active = (patch_now >= 0) & (patch_now < patch_count)
        clipped = jnp.clip(patch_now, 0, patch_count - 1)
        entering = lax.dynamic_index_in_dim(
            acts, jnp.clip(moment, 0, patch_count - 1), 0, keepdims=False
        )
        current = jnp.where(position == 0, entering, arriving)
        rim_pairs = extended(make_pairs(current, gain_key, gain_value), (("height", 0),), tile_rows)
        previous = lax.dynamic_index_in_dim(held, clipped, 0, keepdims=False)
        held = lax.dynamic_update_index_in_dim(
            held, jnp.where(active, rim_pairs, previous), clipped, 0
        )
        listing = lax.dynamic_index_in_dim(listings, clipped, 0, keepdims=False)
        live_count = lax.dynamic_index_in_dim(live_counts, clipped, 0, keepdims=False)
        result = lax.cond(
            active,
            lambda operand: attend(operand, held, listing, live_count, gain_query),
            lambda operand: operand,
            current,
        )
        finishing = active & (position == section_count - 1)
        stored = lax.dynamic_index_in_dim(gathered_out, clipped, 0, keepdims=False)
        gathered_out = lax.dynamic_update_index_in_dim(
            gathered_out, jnp.where(finishing, result, stored), clipped, 0
        )
        outgoing = passed_along(result, "section", 1)
        return (outgoing, held, gathered_out)

    incoming, candidates, collected = lax.fori_loop(
        0, patch_count + section_count - 1, advance, (incoming, candidates, collected)
    )
    latent_out = lax.psum_scatter(
        collected.astype(jnp.float32).astype(jnp.bfloat16),
        "section",
        scatter_dimension=0,
        tiled=True,
    )
    kv_cache = candidates[:, tile_rows : 2 * tile_rows, :][None]
    return (latent_out, kv_cache)


def solution(mesh):
    return jax.shard_map(
        body,
        mesh=mesh,
        in_specs=(
            P(None, "height", None),
            P("section", None, "height", None),
            P("section"),
            P(),
            P(None, "height", None),
            P(None, "height"),
        ),
        out_specs=(P("section", "height", None), P("section", None, "height", None)),
        check_vma=False,
    )
```

profile of v0, /device:TPU:27, one launch (start us, length us, event | category | flops | bytes accessed | tf_op | source)
XLA Modules:
  0.0 1352.8 jit_solution(4099425663827336268)
XLA Ops:
  14.2 109.2 %collective-permute-done.4 = bf16[16,32,5120]{2,1,0:T(8,128)(2,1)} collective-permute-done((bf16[16,32,5120]{2,1,0:T(8,128)(2,1)}, bf16[16,32,5120]{2,1,0:T(8,128)(2,1)}, u32[]{:S(2)}, u32[]{:S(2)}) %collective-permute-start.4) | collective-permute-done | bytes 5242912 | tf_op jit(solution)/shard_map/ppermute | solution.py:20
  125.2 13.0 pad_maximum_fusion.1
  140.0 1157.0 %while.18 = (s32[]{:T(128)}, bf16[32,2560]{1,0:T(8,128)(2,1)S(1)}, bf16[16,96,5120]{2,1,0:T(8,128)(2,1)}, bf16[16,32,2560]{2,1,0:T(8,128)(2,1)}, s32[]{:T(128)},...) while((s32[]{:T(128)}, bf16[32,2560]{1,0:T(8,128)(2,1)S(1)}, ...), condition=%wide.region_7.8_spmd, body=%wide.region_0.7_spmd.sunk | while | flops 136317504 | bytes 57238276 | solution.py:112
  300.9 178.4 %collective-permute-done.2 = bf16[32,2560]{1,0:T(8,128)(2,1)S(1)} collective-permute-done((bf16[32,2560]{1,0:T(8,128)(2,1)S(1)}, bf16[32,2560]{1,0:T(8,128)(2,1)S(1)}, u32[]{:S(2)}, u32[]{:S(2)}) %collective-permute-start.2) | collective-permute-done | bytes 163872 | tf_op jit(solution)/shard_map/while/body/eval_jaxpr/ppermute | solution.py:28
  495.2 26.9 %conditional.2 = (bf16[32,2560]{1,0:T(8,128)(2,1)S(1)}) conditional(s32[]{:T(128)} %convert_element_type.87, bf16[32,2560]{1,0:T(8,128)(2,1)S(1)} %get-tuple-element.417, (bf16[32,2560]{1,0:T(8,128)(2,1)S(1)}, s32[16,12]{1,0:T(8,128)S(1)}, s32[]{:T(128)}, bf16[16,96,5120]{2,1,0:T(8,128)(2,1)}, s32[16]{0:T(128)S(1)}, ...), branch_computations={%region_2.2_spmd, %region_3.6_spmd} | conditional | flops 130337304 | bytes 48532316 | solution.py:98
  496.9 8.3 gather_fusion
  545.6 26.9 %conditional.2 = (bf16[32,2560]{1,0:T(8,128)(2,1)S(1)}) conditional(s32[]{:T(128)} %convert_element_type.87, bf16[32,2560]{1,0:T(8,128)(2,1)S(1)} %get-tuple-element.417, (bf16[32,2560]{1,0:T(8,128)(2,1)S(1)}, s32[16,12]{1,0:T(8,128)S(1)}, s32[]{:T(128)}, bf16[16,96,5120]{2,1,0:T(8,128)(2,1)}, s32[16]{0:T(128)S(1)}, ...), branch_computations={%region_2.2_spmd, %region_3.6_spmd} | conditional | flops 130337304 | bytes 48532316 | solution.py:98
  547.4 8.3 gather_fusion
  596.9 26.9 %conditional.2 = (bf16[32,2560]{1,0:T(8,128)(2,1)S(1)}) conditional(s32[]{:T(128)} %convert_element_type.87, bf16[32,2560]{1,0:T(8,128)(2,1)S(1)} %get-tuple-element.417, (bf16[32,2560]{1,0:T(8,128)(2,1)S(1)}, s32[16,12]{1,0:T(8,128)S(1)}, s32[]{:T(128)}, bf16[16,96,5120]{2,1,0:T(8,128)(2,1)}, s32[16]{0:T(128)S(1)}, ...), branch_computations={%region_2.2_spmd, %region_3.6_spmd} | conditional | flops 130337304 | bytes 48532316 | solution.py:98
  598.7 8.3 gather_fusion
  649.0 26.9 %conditional.2 = (bf16[32,2560]{1,0:T(8,128)(2,1)S(1)}) conditional(s32[]{:T(128)} %convert_element_type.87, bf16[32,2560]{1,0:T(8,128)(2,1)S(1)} %get-tuple-element.417, (bf16[32,2560]{1,0:T(8,128)(2,1)S(1)}, s32[16,12]{1,0:T(8,128)S(1)}, s32[]{:T(128)}, bf16[16,96,5120]{2,1,0:T(8,128)(2,1)}, s32[16]{0:T(128)S(1)}, ...), branch_computations={%region_2.2_spmd, %region_3.6_spmd} | conditional | flops 130337304 | bytes 48532316 | solution.py:98
  700.6 26.9 %conditional.2 = (bf16[32,2560]{1,0:T(8,128)(2,1)S(1)}) conditional(s32[]{:T(128)} %convert_element_type.87, bf16[32,2560]{1,0:T(8,128)(2,1)S(1)} %get-tuple-element.417, (bf16[32,2560]{1,0:T(8,128)(2,1)S(1)}, s32[16,12]{1,0:T(8,128)S(1)}, s32[]{:T(128)}, bf16[16,96,5120]{2,1,0:T(8,128)(2,1)}, s32[16]{0:T(128)S(1)}, ...), branch_computations={%region_2.2_spmd, %region_3.6_spmd} | conditional | flops 130337304 | bytes 48532316 | solution.py:98
  752.1 26.9 %conditional.2 = (bf16[32,2560]{1,0:T(8,128)(2,1)S(1)}) conditional(s32[]{:T(128)} %convert_element_type.87, bf16[32,2560]{1,0:T(8,128)(2,1)S(1)} %get-tuple-element.417, (bf16[32,2560]{1,0:T(8,128)(2,1)S(1)}, s32[16,12]{1,0:T(8,128)S(1)}, s32[]{:T(128)}, bf16[16,96,5120]{2,1,0:T(8,128)(2,1)}, s32[16]{0:T(128)S(1)}, ...), branch_computations={%region_2.2_spmd, %region_3.6_spmd} | conditional | flops 130337304 | bytes 48532316 | solution.py:98
  803.5 26.9 %conditional.2 = (bf16[32,2560]{1,0:T(8,128)(2,1)S(1)}) conditional(s32[]{:T(128)} %convert_element_type.87, bf16[32,2560]{1,0:T(8,128)(2,1)S(1)} %get-tuple-element.417, (bf16[32,2560]{1,0:T(8,128)(2,1)S(1)}, s32[16,12]{1,0:T(8,128)S(1)}, s32[]{:T(128)}, bf16[16,96,5120]{2,1,0:T(8,128)(2,1)}, s32[16]{0:T(128)S(1)}, ...), branch_computations={%region_2.2_spmd, %region_3.6_spmd} | conditional | flops 130337304 | bytes 48532316 | solution.py:98
  854.9 26.9 %conditional.2 = (bf16[32,2560]{1,0:T(8,128)(2,1)S(1)}) conditional(s32[]{:T(128)} %convert_element_type.87, bf16[32,2560]{1,0:T(8,128)(2,1)S(1)} %get-tuple-element.417, (bf16[32,2560]{1,0:T(8,128)(2,1)S(1)}, s32[16,12]{1,0:T(8,128)S(1)}, s32[]{:T(128)}, bf16[16,96,5120]{2,1,0:T(8,128)(2,1)}, s32[16]{0:T(128)S(1)}, ...), branch_computations={%region_2.2_spmd, %region_3.6_spmd} | conditional | flops 130337304 | bytes 48532316 | solution.py:98
  906.7 26.9 %conditional.2 = (bf16[32,2560]{1,0:T(8,128)(2,1)S(1)}) conditional(s32[]{:T(128)} %convert_element_type.87, bf16[32,2560]{1,0:T(8,128)(2,1)S(1)} %get-tuple-element.417, (bf16[32,2560]{1,0:T(8,128)(2,1)S(1)}, s32[16,12]{1,0:T(8,128)S(1)}, s32[]{:T(128)}, bf16[16,96,5120]{2,1,0:T(8,128)(2,1)}, s32[16]{0:T(128)S(1)}, ...), branch_computations={%region_2.2_spmd, %region_3.6_spmd} | conditional | flops 130337304 | bytes 48532316 | solution.py:98
  958.4 26.9 %conditional.2 = (bf16[32,2560]{1,0:T(8,128)(2,1)S(1)}) conditional(s32[]{:T(128)} %convert_element_type.87, bf16[32,2560]{1,0:T(8,128)(2,1)S(1)} %get-tuple-element.417, (bf16[32,2560]{1,0:T(8,128)(2,1)S(1)}, s32[16,12]{1,0:T(8,128)S(1)}, s32[]{:T(128)}, bf16[16,96,5120]{2,1,0:T(8,128)(2,1)}, s32[16]{0:T(128)S(1)}, ...), branch_computations={%region_2.2_spmd, %region_3.6_spmd} | conditional | flops 130337304 | bytes 48532316 | solution.py:98
  1009.6 26.9 %conditional.2 = (bf16[32,2560]{1,0:T(8,128)(2,1)S(1)}) conditional(s32[]{:T(128)} %convert_element_type.87, bf16[32,2560]{1,0:T(8,128)(2,1)S(1)} %get-tuple-element.417, (bf16[32,2560]{1,0:T(8,128)(2,1)S(1)}, s32[16,12]{1,0:T(8,128)S(1)}, s32[]{:T(128)}, bf16[16,96,5120]{2,1,0:T(8,128)(2,1)}, s32[16]{0:T(128)S(1)}, ...), branch_computations={%region_2.2_spmd, %region_3.6_spmd} | conditional | flops 130337304 | bytes 48532316 | solution.py:98
  1061.0 26.9 %conditional.2 = (bf16[32,2560]{1,0:T(8,128)(2,1)S(1)}) conditional(s32[]{:T(128)} %convert_element_type.87, bf16[32,2560]{1,0:T(8,128)(2,1)S(1)} %get-tuple-element.417, (bf16[32,2560]{1,0:T(8,128)(2,1)S(1)}, s32[16,12]{1,0:T(8,128)S(1)}, s32[]{:T(128)}, bf16[16,96,5120]{2,1,0:T(8,128)(2,1)}, s32[16]{0:T(128)S(1)}, ...), branch_computations={%region_2.2_spmd, %region_3.6_spmd} | conditional | flops 130337304 | bytes 48532316 | solution.py:98
  1112.7 26.9 %conditional.2 = (bf16[32,2560]{1,0:T(8,128)(2,1)S(1)}) conditional(s32[]{:T(128)} %convert_element_type.87, bf16[32,2560]{1,0:T(8,128)(2,1)S(1)} %get-tuple-element.417, (bf16[32,2560]{1,0:T(8,128)(2,1)S(1)}, s32[16,12]{1,0:T(8,128)S(1)}, s32[]{:T(128)}, bf16[16,96,5120]{2,1,0:T(8,128)(2,1)}, s32[16]{0:T(128)S(1)}, ...), branch_computations={%region_2.2_spmd, %region_3.6_spmd} | conditional | flops 130337304 | bytes 48532316 | solution.py:98
  1164.2 26.9 %conditional.2 = (bf16[32,2560]{1,0:T(8,128)(2,1)S(1)}) conditional(s32[]{:T(128)} %convert_element_type.87, bf16[32,2560]{1,0:T(8,128)(2,1)S(1)} %get-tuple-element.417, (bf16[32,2560]{1,0:T(8,128)(2,1)S(1)}, s32[16,12]{1,0:T(8,128)S(1)}, s32[]{:T(128)}, bf16[16,96,5120]{2,1,0:T(8,128)(2,1)}, s32[16]{0:T(128)S(1)}, ...), branch_computations={%region_2.2_spmd, %region_3.6_spmd} | conditional | flops 130337304 | bytes 48532316 | solution.py:98
  1215.4 26.9 %conditional.2 = (bf16[32,2560]{1,0:T(8,128)(2,1)S(1)}) conditional(s32[]{:T(128)} %convert_element_type.87, bf16[32,2560]{1,0:T(8,128)(2,1)S(1)} %get-tuple-element.417, (bf16[32,2560]{1,0:T(8,128)(2,1)S(1)}, s32[16,12]{1,0:T(8,128)S(1)}, s32[]{:T(128)}, bf16[16,96,5120]{2,1,0:T(8,128)(2,1)}, s32[16]{0:T(128)S(1)}, ...), branch_computations={%region_2.2_spmd, %region_3.6_spmd} | conditional | flops 130337304 | bytes 48532316 | solution.py:98
  1266.8 26.9 %conditional.2 = (bf16[32,2560]{1,0:T(8,128)(2,1)S(1)}) conditional(s32[]{:T(128)} %convert_element_type.87, bf16[32,2560]{1,0:T(8,128)(2,1)S(1)} %get-tuple-element.417, (bf16[32,2560]{1,0:T(8,128)(2,1)S(1)}, s32[16,12]{1,0:T(8,128)S(1)}, s32[]{:T(128)}, bf16[16,96,5120]{2,1,0:T(8,128)(2,1)}, s32[16]{0:T(128)S(1)}, ...), branch_computations={%region_2.2_spmd, %region_3.6_spmd} | conditional | flops 130337304 | bytes 48532316 | solution.py:98
  1302.3 43.7 %reduce-scatter.2.cloned.1.call-done = bf16[2,32,2560]{2,1,0:T(8,128)(2,1)} async-done(((bf16[16,32,2560]{2,1,0:T(8,128)(2,1)}), bf16[2,32,2560]{2,1,0:T(8,128)(2,1)}) %reduce-scatter.2.cloned.1.call-update) | async-done | bytes 327696 | tf_op jit(solution)/shard_map/reduce_scatter | solution.py:115
  (637 shorter events, 966.5 us)
Async XLA Ops:
  7.2 1338.8 %reduce-scatter.2.cloned.1.call-start = ((), (), s32[]{:S(2)}) async-start(), calls=%async_computation.1 | async-start | bytes 2949120 | tf_op jit(solution)/shard_map/reduce_scatter | solution.py:115
  7.2 116.1 %collective-permute-start.4 = (bf16[16,32,5120]{2,1,0:T(8,128)(2,1)}, bf16[16,32,5120]{2,1,0:T(8,128)(2,1)}, u32[]{:S(2)}, u32[]{:S(2)}) collective-permute-start(bf16[16,32,5120]{2,1,0:T(8,128)(2,1)} %bitcast.75), channel_id=1, source_target_pairs={{1,0},{2,1},{3,2},{4,3},{5,4},{6,5},{7,6},{8,7},{9,8},{10,9},{11,1... | collective-permute-start | bytes 15728648 | tf_op jit(solution)/shard_map/ppermute | solution.py:20
  9.4 115.8 %collective-permute-start.3 = (bf16[16,32,5120]{2,1,0:T(8,128)(2,1)}, bf16[16,32,5120]{2,1,0:T(8,128)(2,1)}, u32[]{:S(2)}, u32[]{:S(2)}) collective-permute-start(bf16[16,32,5120]{2,1,0:T(8,128)(2,1)} %bitcast.76), channel_id=1, source_target_pairs={{0,1},{1,2},{2,3},{3,4},{4,5},{5,6},{6,7},{7,8},{8,9},{9,10},{10,1... | collective-permute-start | bytes 15728648 | tf_op jit(solution)/shard_map/ppermute | solution.py:17
  141.3 9.2 collective-permute-start.1
  144.4 9.8 collective-permute-start
  163.5 10.2 collective-permute-start.1
  169.7 9.9 collective-permute-start
  194.8 8.5 collective-permute-start
  218.2 8.5 collective-permute-start
  298.9 180.4 %collective-permute-start.2 = (bf16[32,2560]{1,0:T(8,128)(2,1)S(1)}, bf16[32,2560]{1,0:T(8,128)(2,1)S(1)}, u32[]{:S(2)}, u32[]{:S(2)}) collective-permute-start(bf16[32,2560]{1,0:T(8,128)(2,1)S(1)} %get-tuple-element.472), channel_id=1, source_target_pairs={{0,32},{32,64},{64,96},{96,128},{128,160},{160,192},{192,224},{1,3... | collective-permute-start | bytes 491528 | tf_op jit(solution)/shard_map/while/body/eval_jaxpr/ppermute | solution.py:28
  584.9 9.6 collective-permute-start
  636.5 10.1 collective-permute-start
  688.6 9.5 collective-permute-start
  740.1 9.5 collective-permute-start
  791.7 9.4 collective-permute-start
  843.1 9.4 collective-permute-start
  894.6 9.6 collective-permute-start
  946.3 9.6 collective-permute-start
  997.9 9.2 collective-permute-start
  1049.2 9.4 collective-permute-start
  1100.6 9.6 collective-permute-start
  1152.3 9.3 collective-permute-start
  1203.7 9.3 collective-permute-start
  1255.0 9.4 collective-permute-start
  (66 other events, 532.7 us)
Sparse Core Ops, SparseCore 0:
  1297.1 48.8 reduce-scatter.1
where the time goes:
time: 1360 us; the launch traced here: 1350 us
  waiting for transfers between devices  597 us (44%)
  local copies, waits for them, and re-layouts  328 us (24%)
  other arithmetic  188 us (14%)
  starting transfers between devices  165 us (12%)
  matrix products  57.4 us (4%)
  between operations  14.7 us (1%)
    ppermute x23, waiting for transfers between devices, passed_along(): lax.ppermute(value, axis, [(source, source + steps) for source in range(f...  297 us
    gather x32, local copies, waits for them, and re-layouts, attend(): jnp.take(flattened, listing, axis=0)  254 us
    ppermute x24, waiting for transfers between devices, extended(): lax.ppermute(lax.slice_in_dim(block, 0, width, axis=dim), axis, backward)  223 us
    ppermute x24, starting transfers between devices, extended(): lax.ppermute(lax.slice_in_dim(block, block.shape[dim] - width, None, axis...  88.9 us
    dynamic_update_slice x23, other arithmetic, advance(): lax.dynamic_update_index_in_dim(held, jnp.where(active, rim_pairs, previo...  56.8 us
    select_n x32, other arithmetic, attend(): jnp.take(flattened, listing, axis=0)  53.6 us
    ppermute x24, starting transfers between devices, extended(): lax.ppermute(lax.slice_in_dim(block, 0, width, axis=dim), axis, backward)  46.6 us
    reduce_scatter x1, waiting for transfers between devices, body(): lax.psum_scatter(collected.astype(jnp.float32).astype(jnp.bfloat16), 'sec...  43.7 us
  transfers between devices with their start and end apart: 72, of which 72 were waited for; matrix products, arithmetic and copies ran while one was open for 3% of the time, Pallas kernels for 0%

commit v1 on v0

v1 whole, which is shorter than its diff:
```python
import functools
import math

import jax
import jax.numpy as jnp
from jax import lax
from jax.experimental import pallas as pl
from jax.experimental.pallas import tpu as pltpu
from jax.sharding import PartitionSpec as P

HEAD_DIM = 128
BLOCK = 2
PAIR = 2 * HEAD_DIM
SCALE = 1.0 / math.sqrt(HEAD_DIM)
NEVER = -1e30
VMEM = 56 * 1024 * 1024


def normalized(tile):
    wide = tile.astype(jnp.float32)
    return wide * (1.0 / jnp.sqrt(jnp.mean(wide * wide, axis=-1, keepdims=True) + 1e-06))


def split_heads(pair):
    zeros = jnp.zeros((pair.shape[0], HEAD_DIM), pair.dtype)
    return jnp.concatenate(
        [
            jnp.concatenate([pair[:, :HEAD_DIM], zeros], axis=1),
            jnp.concatenate([zeros, pair[:, HEAD_DIM:]], axis=1),
        ],
        axis=0,
    )


def joined_heads(both):
    rows = both.shape[0] // 2
    return jnp.concatenate([both[:rows, :HEAD_DIM], both[rows:, HEAD_DIM:]], axis=1)


def products(queries, keys):
    return lax.dot_general(
        queries, keys, (((1,), (1,)), ((), ())), preferred_element_type=jnp.float32
    )


def pairs_of(normed, gains_ref):
    channels = normed.shape[-1]
    return (
        (normed * gains_ref[:, channels : 2 * channels]).astype(jnp.bfloat16),
        (normed * gains_ref[:, 2 * channels :]).astype(jnp.bfloat16),
    )


def own_kernel(
    where_ref,
    self_ref,
    past_low,
    old_own,
    past_high,
    next_own,
    second_own,
    third_own,
    next_low,
    next_high,
    later_low,
    later_high,
    gains_ref,
    bias_even,
    bias_odd,
    cache_in,
    queries_ref,
    fresh_ref,
    mixed_ref,
    highest_ref,
    total_ref,
    cache_ref,
    sent,
    old_low,
    old_high,
    even_scores,
    odd_scores,
    even_weights,
    odd_weights,
):
    del cache_in
    channels = self_ref.shape[-1]
    pairs = channels // PAIR
    active = where_ref[1] > 0

    @pl.when(active)
    def _():
        for i in range(BLOCK):
            normed = normalized(self_ref[i])
            queries_ref[i] = (normed * gains_ref[:, :channels]).astype(jnp.bfloat16)
            fresh_ref[i, :, :channels], fresh_ref[i, :, channels:] = pairs_of(normed, gains_ref)
        writing = pltpu.make_async_copy(
            fresh_ref, cache_ref.at[pl.ds(where_ref[0] * BLOCK, BLOCK)], sent
        )
        writing.start()
        for past, old in ((past_low, old_low), (past_high, old_high)):
            for i in range(BLOCK):
                normed = normalized(past[i])
                old[i, :, :channels], old[i, :, channels:] = pairs_of(normed, gains_ref)

        def tiles_of(i, cut):
            old = [ref[j, :, cut] for j in range(i, BLOCK) for ref in (old_low, old_own, old_high)]
            fresh = [fresh_ref[j, :, cut] for j in range(i + 1)]
            near = [next_low[0, :, cut], next_own[0, :, cut], next_high[0, :, cut]]
            second = [later_low[0, :, cut], second_own[0, :, cut], later_high[0, :, cut]]
            third = [later_low[1, :, cut], third_own[0, :, cut], later_high[1, :, cut]]
            return jnp.concatenate(
                old + fresh + (near + second if i == 0 else second + third), axis=0
            )

        sides = ((even_scores, even_weights, bias_even), (odd_scores, odd_weights, bias_odd))
        for pair in range(pairs):
            cut = slice(pair * PAIR, (pair + 1) * PAIR)
            for i, (scores_ref, _, _) in enumerate(sides):
                scores_ref[pair] = products(
                    split_heads(queries_ref[i, :, cut]), tiles_of(i, cut)
                )
        for pair in range(pairs):
            for i, (scores_ref, weights_ref, bias) in enumerate(sides):
                scores = scores_ref[pair] * SCALE + bias[0]
                highest = jnp.max(scores, axis=-1, keepdims=True)
                exponent = jnp.exp(scores - highest)
                highest_ref[i, :, pair : pair + 1] = highest
                total_ref[i, :, pair : pair + 1] = jnp.sum(exponent, axis=-1, keepdims=True)
                weights_ref[pair] = exponent.astype(jnp.bfloat16)
        for pair in range(pairs):
            cut = slice(pair * PAIR, (pair + 1) * PAIR)
            value_cut = slice(channels + pair * PAIR, channels + (pair + 1) * PAIR)
            for i, (_, weights_ref, _) in enumerate(sides):
                mixed_ref[i, :, cut] = joined_heads(
                    jnp.dot(
                        weights_ref[pair],
                        tiles_of(i, value_cut),
                        preferred_element_type=jnp.float32,
                    )
                )
        writing.wait()

    @pl.when(jnp.logical_not(active))
    def _():
        fresh_ref[...] = jnp.zeros_like(fresh_ref)


def side_kernel(where_ref, *refs, relayed):
    (
        self_ref,
        low_ref,
        high_ref,
        queries_ref,
        mixed_ref,
        highest_ref,
        total_ref,
        gains_ref,
        bias_ref,
    ) = refs[:9]
    entering_ref = refs[9] if relayed else None
    result_ref, keys, values, scores_ref, weights_ref, shrink_ref = refs[-6:]
    channels = self_ref.shape[-1]
    rows = self_ref.shape[1]
    pairs = channels // PAIR
    active = where_ref[1] > 0
    last = where_ref[2] > 0

    @pl.when(active)
    def _():
        for side, source in enumerate((low_ref, high_ref)):
            for i in range(BLOCK):
                at = pl.ds((side * BLOCK + i) * rows, rows)
                keys[at, :], values[at, :] = pairs_of(normalized(source[i]), gains_ref)
        bias = jnp.concatenate(
            [
                jnp.broadcast_to(bias_ref[0, i : i + 1], (2 * rows, bias_ref.shape[-1]))
                for i in range(BLOCK)
            ],
            axis=0,
        )
        for pair in range(pairs):
            cut = slice(pair * PAIR, (pair + 1) * PAIR)
            both = jnp.concatenate(
                [split_heads(queries_ref[i, :, cut]) for i in range(BLOCK)], axis=0
            )
            scores_ref[pair] = products(both, keys[:, cut])
        for pair in range(pairs):
            scores = scores_ref[pair] * SCALE + bias
            column = slice(pair, pair + 1)
            before = jnp.concatenate([highest_ref[i, :, column] for i in range(BLOCK)], axis=0)
            sums = jnp.concatenate([total_ref[i, :, column] for i in range(BLOCK)], axis=0)
            highest = jnp.maximum(before, jnp.max(scores, axis=-1, keepdims=True))
            exponent = jnp.exp(scores - highest)
            shrink = jnp.exp(before - highest)
            inverse = 1.0 / (sums * shrink + jnp.sum(exponent, axis=-1, keepdims=True))
            weights_ref[pair] = (exponent * inverse).astype(jnp.bfloat16)
            shrink_ref[pair] = jnp.broadcast_to(shrink * inverse, (BLOCK * 2 * rows, HEAD_DIM))
        for pair in range(pairs):
            cut = slice(pair * PAIR, (pair + 1) * PAIR)
            added = jnp.dot(
                weights_ref[pair], values[:, cut], preferred_element_type=jnp.float32
            )
            shrink = shrink_ref[pair]
            for i in range(BLOCK):
                top = 2 * rows * i
                kept = mixed_ref[i, :, cut] * jnp.concatenate(
                    [shrink[top : top + rows], shrink[top + rows : top + 2 * rows]], axis=1
                )
                result_ref[i, :, cut] = (
                    self_ref[i, :, cut].astype(jnp.float32)
                    + kept
                    + joined_heads(added[top : top + 2 * rows])
                ).astype(jnp.bfloat16)

    if relayed:

        @pl.when(last)
        def _():
            result_ref[...] = entering_ref[...]

    @pl.when(jnp.logical_not(active | last) if relayed else jnp.logical_not(active))
    def _():
        result_ref[...] = jnp.zeros_like(result_ref)


def whole(shape):
    return pl.BlockSpec(shape, lambda i, w: (0,) * len(shape))


def at_block(shape):
    return pl.BlockSpec((1,) + shape, lambda i, w: (w[0],) + (0,) * len(shape))


def own_part(where, tile, old, stale, near, far, gains, biases, cache):
    patches, rows, pair_channels = stale.shape
    channels = pair_channels // 2

    def at_patch(shift):
        return pl.BlockSpec(
            (1, rows, pair_channels),
            lambda i, w: (jnp.minimum(w[0] * BLOCK + shift, patches - 1), 0, 0),
        )

    pairs = whole((BLOCK, rows, pair_channels))
    block = whole((BLOCK, rows, channels))
    stats = whole((BLOCK, 2 * rows, HEAD_DIM))
    second = pl.BlockSpec((1, rows, pair_channels), lambda i, w: (1, 0, 0))
    even, odd = biases[0].shape[-1], biases[1].shape[-1]
    count = channels // PAIR
    return pl.pallas_call(
        own_kernel,
        grid_spec=pltpu.PrefetchScalarGridSpec(
            num_scalar_prefetch=1,
            grid=(1,),
            in_specs=[block, block, pairs, block]
            + [at_patch(1), at_patch(2), at_patch(3)]
            + [second, second, pairs, pairs]
            + [whole(gains.shape), at_block((1, even)), at_block((1, odd))]
            + [pl.BlockSpec(memory_space=pl.ANY)],
            out_specs=[block, pairs, block, stats, stats, pl.BlockSpec(memory_space=pl.ANY)],
            scratch_shapes=[
                pltpu.SemaphoreType.DMA,
                pltpu.VMEM((BLOCK, rows, pair_channels), jnp.bfloat16),
                pltpu.VMEM((BLOCK, rows, pair_channels), jnp.bfloat16),
                pltpu.VMEM((count, 2 * rows, even), jnp.float32),
                pltpu.VMEM((count, 2 * rows, odd), jnp.float32),
                pltpu.VMEM((count, 2 * rows, even), jnp.bfloat16),
                pltpu.VMEM((count, 2 * rows, odd), jnp.bfloat16),
            ],
        ),
        out_shape=[
            jax.ShapeDtypeStruct((BLOCK, rows, channels), jnp.bfloat16),
            jax.ShapeDtypeStruct((BLOCK, rows, pair_channels), jnp.bfloat16),
            jax.ShapeDtypeStruct((BLOCK, rows, channels), jnp.float32),
            jax.ShapeDtypeStruct((BLOCK, 2 * rows, HEAD_DIM), jnp.float32),
            jax.ShapeDtypeStruct((BLOCK, 2 * rows, HEAD_DIM), jnp.float32),
            jax.ShapeDtypeStruct(cache.shape, jnp.bfloat16),
        ],
        input_output_aliases={15: 5},
        compiler_params=pltpu.CompilerParams(vmem_limit_bytes=VMEM),
        cost_estimate=pl.CostEstimate(
            flops=8 * rows * (even + odd) * channels, bytes_accessed=16000000, transcendentals=0
        ),
    )(where, tile, *old, stale, stale, stale, near[0], near[1], far[0], far[1], gains, *biases, cache)


def side_part(where, tile, low, high, queries, mixed, highest, total, gains, bias, entering):
    rows, channels = tile.shape[1:]
    block = whole((BLOCK, rows, channels))
    stats = whole((BLOCK, 2 * rows, HEAD_DIM))
    keys = bias.shape[-1]
    count = channels // PAIR
    relayed = entering is not None
    return pl.pallas_call(
        functools.partial(side_kernel, relayed=relayed),
        grid_spec=pltpu.PrefetchScalarGridSpec(
            num_scalar_prefetch=1,
            grid=(1,),
            in_specs=[block] * 5
            + [stats] * 2
            + [whole(gains.shape), at_block((BLOCK, keys))]
            + [block] * relayed,
            out_specs=block,
            scratch_shapes=[
                pltpu.VMEM((keys, channels), jnp.bfloat16),
                pltpu.VMEM((keys, channels), jnp.bfloat16),
                pltpu.VMEM((count, 2 * BLOCK * rows, keys), jnp.float32),
                pltpu.VMEM((count, 2 * BLOCK * rows, keys), jnp.bfloat16),
                pltpu.VMEM((count, 2 * BLOCK * rows, HEAD_DIM), jnp.float32),
            ],
        ),
        out_shape=jax.ShapeDtypeStruct((BLOCK, rows, channels), jnp.bfloat16),
        compiler_params=pltpu.CompilerParams(vmem_limit_bytes=VMEM),
        cost_estimate=pl.CostEstimate(
            flops=16 * rows * keys * channels, bytes_accessed=6000000, transcendentals=0
        ),
    )(
        where, tile, low, high, queries, mixed, highest, total, gains, bias,
        *([entering] if relayed else []),
    )


def hop(value, section_shift, height_shift):
    sections, heights = lax.axis_size("section"), lax.axis_size("height")
    pairs = [
        (
            s * heights + h,
            (s + section_shift) % sections * heights + (h + height_shift) % heights,
        )
        for s in range(sections)
        for h in range(heights)
    ]
    return lax.ppermute(value, ("section", "height"), pairs)


def swapped(value, one, other):
    pairs = [(s, s) for s in range(lax.axis_size("section")) if s not in (one, other)]
    return lax.ppermute(value, "section", pairs + [(one, other), (other, one)])


def key_biases(tile_lists, tile_counts, rows):
    lists = tile_lists[:, 0, :]
    patches = lists.shape[0]
    live = jnp.arange(lists.shape[1], dtype=jnp.int32)[None, :] < tile_counts
    wanted = (
        3 * (jnp.arange(patches, dtype=jnp.int32) - 2)[:, None]
        + jnp.arange(15, dtype=jnp.int32)[None, :]
    )
    listed = jnp.any((lists[:, :, None] == wanted[:, None, :]) & live[:, :, None], axis=1)
    listed = listed.reshape(patches // BLOCK, BLOCK, 15)

    def bias(i, columns):
        chosen = jnp.stack(
            [listed[:, i, c] if c >= 0 else jnp.zeros_like(listed[:, i, 0]) for c in columns], axis=1
        )
        chosen = jnp.repeat(chosen, rows, axis=1)
        return jnp.where(chosen, 0.0, NEVER).astype(jnp.float32)[:, None, :]

    even = bias(0, (0, 1, 2, 3, 4, 5, 7, 9, 10, 11, 12, 13, 14))
    odd = bias(1, (0, 1, 2, 4, 7, 9, 10, 11, 12, 13, 14))
    side = jnp.concatenate([bias(0, (6, -1, 8, -1)), bias(1, (3, 6, 5, 8))], axis=1)
    return (even, odd), side


def body(acts, stale, layer_ids, layer_gains, tile_lists, tile_counts):
    sections = lax.axis_size("section")
    position = lax.axis_index("section")
    patches, rows, channels = acts.shape
    blocks = patches // BLOCK
    stale = stale[0]
    gains = lax.dynamic_slice_in_dim(layer_gains, layer_ids[0], 1, 0).astype(jnp.float32)
    biases, side_bias = key_biases(tile_lists, tile_counts, rows)
    acts = acts.reshape(blocks, BLOCK, rows, channels)

    def halo_of(moment, after=None):
        first = BLOCK * (moment - position + 1)
        if after is not None:
            first, _ = lax.optimization_barrier((first, after))
        sent = lax.dynamic_slice_in_dim(stale, jnp.clip(first, 0, patches - BLOCK), BLOCK, 0)
        return [hop(sent, 0, 1), hop(sent, 0, -1)]

    def relay(payload):
        return [hop(payload, 1, shift) for shift in (0, 1, -1)]

    moments = blocks + sections - 1
    own = jnp.zeros((BLOCK, rows, 2 * channels), jnp.bfloat16)
    past_low = past_high = jnp.zeros((BLOCK, rows, channels), jnp.bfloat16)
    cache = jnp.zeros(stale.shape, jnp.bfloat16)
    tile, low, high = relay(acts[0])
    halos = [halo_of(-1), halo_of(0), halo_of(1)]
    latent = None
    for moment in range(moments):
        block = moment - position
        where = jnp.stack(
            [
                jnp.clip(block, 0, blocks - 1),
                ((block >= 0) & (block < blocks)).astype(jnp.int32),
                (position == sections - 1).astype(jnp.int32),
            ]
        )
        queries, own, mixed, highest, total, cache = own_part(
            where,
            tile,
            (past_low, own, past_high),
            stale,
            halos[moment],
            halos[moment + 1],
            gains,
            biases,
            cache,
        )
        entering = acts[moment + 1] if moment + 1 < blocks else None
        result = side_part(
            where, tile, low, high, queries, mixed, highest, total, gains, side_bias, entering
        )
        past_low, past_high = low, high
        if moment + 1 < moments:
            tile, low, high = relay(result)
            if moment + 2 < moments - 1:
                halos.append(halo_of(moment + 2, result[0, 0, 0]))
            else:
                halos.append(halos[-1])
        owner = moment - (sections - 1)
        if owner >= 0:
            arrived = swapped(result, sections - 1, owner) if owner < sections - 1 else result
            latent = arrived if latent is None else jnp.where(position == owner, arrived, latent)
    return (latent, cache[None])


def solution(mesh):
    return jax.shard_map(
        body,
        mesh=mesh,
        in_specs=(
            P(None, "height", None),
            P("section", None, "height", None),
            P("section"),
            P(),
            P(None, "height", None),
            P(None, "height"),
        ),
        out_specs=(P("section", "height", None), P("section", None, "height", None)),
        check_vma=False,
    )
```

time: 1360 us -> 521 us (0.38)
  waiting for transfers between devices: 597 us -> 73.6 us
  local copies, waits for them, and re-layouts: 328 us -> 34.1 us
  other arithmetic: 188 us -> 13.4 us
  Pallas kernels: 0 us -> 150 us
  starting transfers between devices: 165 us -> 237 us
  matrix products: 57.4 us -> 0 us
    ppermute x71 -> x82, waiting for transfers between devices: 553 us -> 73.6 us  [the longest x75 73.6 us: hop(): return lax.ppermute(value, ('section', 'height'), pairs)]
    gather x32 -> x0, local copies, waits for them, and re-layouts: 254 us -> none  [attend(): jnp.take(flattened, listing, axis=0)]
    pallas_call x0 -> x30, Pallas kernels: none -> 150 us  [the longest x15 82 us: own_part(): pl.pallas_call(own_kernel, grid_spec=pltpu.PrefetchScalarGridSpec(num_sca...]
    dynamic_update_slice x46 -> x0, other arithmetic: 73.2 us -> none  [the longest x23 56.8 us: advance(): lax.dynamic_update_index_in_dim(held, jnp.where(active, rim_pairs, previo...]
    ppermute x71 -> x82, starting transfers between devices: 165 us -> 237 us  [the longest x75 206 us: hop(): return lax.ppermute(value, ('section', 'height'), pairs)]
    dot_general x33 -> x0, matrix products: 57.4 us -> none  [the longest x16 43.6 us: attend(): jnp.einsum('hqk,khd->qhd', weights, picked[:, 1], preferred_element_type=...]
    select_n x32 -> x5, other arithmetic: 53.6 us -> 1.86 us  [the longest x1 1.83 us: body(): jnp.where(position == owner, arrived, latent)]
    reduce_scatter x1 -> x0, waiting for transfers between devices: 43.7 us -> none  [body(): lax.psum_scatter(collected.astype(jnp.float32).astype(jnp.bfloat16), 'sec...]
  transfers between devices with their start and end apart: 72 -> 82, of which waited for: 72 -> 17; matrix products, arithmetic and copies ran while one was open for 3% -> 5% of each run, Pallas kernels for 0% -> 29%
where the time goes in v1:
time: 521 us; the launch traced here: 511 us
  starting transfers between devices  237 us (45%)
  Pallas kernels  150 us (29%)
  waiting for transfers between devices  73.6 us (14%)
  local copies, waits for them, and re-layouts  34.1 us (7%)
  other arithmetic  13.4 us (3%)
    ppermute x75, starting transfers between devices, hop(): return lax.ppermute(value, ('section', 'height'), pairs)  206 us
    pallas_call x15, Pallas kernels, own_part(): pl.pallas_call(own_kernel, grid_spec=pltpu.PrefetchScalarGridSpec(num_sca...  82 us
    ppermute x75, waiting for transfers between devices, hop(): return lax.ppermute(value, ('section', 'height'), pairs)  73.6 us
    pallas_call x15, Pallas kernels, side_part(): pl.pallas_call(functools.partial(side_kernel, relayed=relayed), grid_spec...  68 us
    ppermute x7, starting transfers between devices, swapped(): return lax.ppermute(value, 'section', pairs + [(one, other), (other, one)])  30.8 us
    unnamed x131, local copies, waits for them, and re-layouts  12.9 us
  transfers between devices with their start and end apart: 82, of which 17 were waited for; matrix products, arithmetic and copies ran while one was open for 5% of the time, Pallas kernels for 29%

profile of v1, /device:TPU:27, one launch (start us, length us, event | category | flops | bytes accessed | tf_op | source)
XLA Modules:
  0.0 510.8 jit_solution(12157440505719035680)
XLA Ops:
  0.7 8.1 %dynamic-slice_bitcast_fusion = (bf16[2,32,5120]{2,1,0:T(8,128)(2,1)}, bf16[2,32,5120]{2,1,0:T(8,128)(2,1)}, bf16[2,32,5120]{2,1,0:T(8,128)(2,1)}, bf16[2,32,512...) fusion(bf16[1,16,32,5120]{3,2,1,0:T(8,128)(2,1)} %param.7, ...), kind=kLoop, calls=%fused_computation | loop fusion | bytes 19660860 | tf_op jit(solution)/shard_map/dynamic_slice | solution.py:379
  26.4 7.5 %collective-permute-done.1.refs_1_.past_low = bf16[2,32,2560]{2,1,0:T(8,128)(2,1)S(1)} collective-permute-done((bf16[2,32,2560]{2,1,0:T(8,128)(2,1)S(1)}, bf16[2,32,2560]{2,1,0:T(8,128)(2,1)S(1)}, u32[]{:S(2)}, u32[]{:S(2)}) %collective-permute-start.1) | collective-permute-done | bytes 327712 | tf_op jit(solution)/shard_map/ppermute | solution.py:333
  39.8 6.9 %collective-permute-start.2 = (bf16[2,32,2560]{2,1,0:T(8,128)(2,1)}, bf16[2,32,2560]{2,1,0:T(8,128)(2,1)}, u32[]{:S(2)}, u32[]{:S(2)}) collective-permute-start(bf16[2,32,2560]{2,1,0:T(8,128)(2,1)} %copy-done.53), channel_id=1, source_target_pairs={{0,63},{1,32},{2,33},{3,34},{4,35},{5,36},{6,37},{7,38},{8,39},{9,... | collective-permute-start | bytes 983048 | tf_op jit(solution)/shard_map/ppermute | solution.py:333
  67.5 6.8 %collective-permute-start.7 = (bf16[2,32,2560]{2,1,0:T(8,128)(2,1)}, bf16[2,32,2560]{2,1,0:T(8,128)(2,1)S(1)}, u32[]{:S(2)}, u32[]{:S(2)}) collective-permute-start(bf16[2,32,2560]{2,1,0:T(8,128)(2,1)} %shard_map.81), channel_id=1, source_target_pairs={{0,32},{1,33},{2,34},{3,35},{4,36},{5,37},{6,38},{7,39},{8,40},{9,... | collective-permute-start | bytes 983048 | tf_op jit(solution)/shard_map/ppermute | solution.py:333
  94.6 8.6 %collective-permute-start.12 = (bf16[2,32,2560]{2,1,0:T(8,128)(2,1)}, bf16[2,32,2560]{2,1,0:T(8,128)(2,1)S(1)}, u32[]{:S(2)}, u32[]{:S(2)}) collective-permute-start(bf16[2,32,2560]{2,1,0:T(8,128)(2,1)} %shard_map.83), channel_id=1, source_target_pairs={{0,32},{1,33},{2,34},{3,35},{4,36},{5,37},{6,38},{7,39},{8,40},{9,... | collective-permute-start | bytes 983048 | tf_op jit(solution)/shard_map/ppermute | solution.py:333
  126.5 8.2 %collective-permute-start.17 = (bf16[2,32,2560]{2,1,0:T(8,128)(2,1)}, bf16[2,32,2560]{2,1,0:T(8,128)(2,1)S(1)}, u32[]{:S(2)}, u32[]{:S(2)}) collective-permute-start(bf16[2,32,2560]{2,1,0:T(8,128)(2,1)} %shard_map.85), channel_id=1, source_target_pairs={{0,32},{1,33},{2,34},{3,35},{4,36},{5,37},{6,38},{7,39},{8,40},{9,... | collective-permute-start | bytes 983048 | tf_op jit(solution)/shard_map/ppermute | solution.py:333
  148.3 6.7 %collective-permute-done.19.refs_2_.past_high = bf16[2,32,2560]{2,1,0:T(8,128)(2,1)} collective-permute-done((bf16[2,32,2560]{2,1,0:T(8,128)(2,1)}, bf16[2,32,2560]{2,1,0:T(8,128)(2,1)}, u32[]{:S(2)}, u32[]{:S(2)}) %collective-permute-start.19) | collective-permute-done | bytes 327712 | tf_op jit(solution)/shard_map/ppermute | solution.py:333
  158.1 10.7 %collective-permute-start.22 = (bf16[2,32,2560]{2,1,0:T(8,128)(2,1)}, bf16[2,32,2560]{2,1,0:T(8,128)(2,1)S(1)}, u32[]{:S(2)}, u32[]{:S(2)}) collective-permute-start(bf16[2,32,2560]{2,1,0:T(8,128)(2,1)} %shard_map.87), channel_id=1, source_target_pairs={{0,32},{1,33},{2,34},{3,35},{4,36},{5,37},{6,38},{7,39},{8,40},{9,... | collective-permute-start | bytes 983048 | tf_op jit(solution)/shard_map/ppermute | solution.py:333
  193.8 7.8 %collective-permute-start.27 = (bf16[2,32,2560]{2,1,0:T(8,128)(2,1)}, bf16[2,32,2560]{2,1,0:T(8,128)(2,1)S(1)}, u32[]{:S(2)}, u32[]{:S(2)}) collective-permute-start(bf16[2,32,2560]{2,1,0:T(8,128)(2,1)} %shard_map.89), channel_id=1, source_target_pairs={{0,32},{1,33},{2,34},{3,35},{4,36},{5,37},{6,38},{7,39},{8,40},{9,... | collective-permute-start | bytes 983048 | tf_op jit(solution)/shard_map/ppermute | solution.py:333
  204.9 8.1 %collective-permute-done.27.self_ref.refs_0_ = bf16[2,32,2560]{2,1,0:T(8,128)(2,1)S(1)} collective-permute-done((bf16[2,32,2560]{2,1,0:T(8,128)(2,1)}, bf16[2,32,2560]{2,1,0:T(8,128)(2,1)S(1)}, u32[]{:S(2)}, u32[]{:S(2)}) %collective-permute-start.27) | collective-permute-done | bytes 327712 | tf_op jit(solution)/shard_map/ppermute | solution.py:333
  225.3 9.6 %collective-permute-start.32 = (bf16[2,32,2560]{2,1,0:T(8,128)(2,1)}, bf16[2,32,2560]{2,1,0:T(8,128)(2,1)}, u32[]{:S(2)}, u32[]{:S(2)}) collective-permute-start(bf16[2,32,2560]{2,1,0:T(8,128)(2,1)} %shard_map.91), channel_id=1, source_target_pairs={{0,32},{1,33},{2,34},{3,35},{4,36},{5,37},{6,38},{7,39},{8,40},{9,... | collective-permute-start | bytes 983048 | tf_op jit(solution)/shard_map/ppermute | solution.py:333
  254.6 8.7 %collective-permute-start.37 = (bf16[2,32,2560]{2,1,0:T(8,128)(2,1)}, bf16[2,32,2560]{2,1,0:T(8,128)(2,1)}, u32[]{:S(2)}, u32[]{:S(2)}) collective-permute-start(bf16[2,32,2560]{2,1,0:T(8,128)(2,1)} %shard_map.93), channel_id=1, source_target_pairs={{0,32},{1,33},{2,34},{3,35},{4,36},{5,37},{6,38},{7,39},{8,40},{9,... | collective-permute-start | bytes 983048 | tf_op jit(solution)/shard_map/ppermute | solution.py:333
  274.8 6.5 %shard_map.94 = (bf16[2,32,2560]{2,1,0:T(8,128)(2,1)}, bf16[2,32,5120]{2,1,0:T(8,128)(2,1)}, f32[2,32,2560]{2,1,0:T(8,128)}, f32[2,64,128]{2,1,0:T(8,128)}, f32[...) custom-call(s32[3]{0:T(128)} %add_add_fusion.7.where_ref, ...), custom_call_target="tpu_custom_call", output_to_operand_aliasing={{5}: (15, {})} | custom-call | flops 503316480 | bytes 16000000 | tf_op jit(solution)/shard_map/pallas_call | solution.py:250
  306.2 6.6 %shard_map.96 = (bf16[2,32,2560]{2,1,0:T(8,128)(2,1)}, bf16[2,32,5120]{2,1,0:T(8,128)(2,1)}, f32[2,32,2560]{2,1,0:T(8,128)}, f32[2,64,128]{2,1,0:T(8,128)}, f32[...) custom-call(s32[3]{0:T(128)} %add_add_fusion.6.where_ref, ...), custom_call_target="tpu_custom_call", output_to_operand_aliasing={{5}: (15, {})} | custom-call | flops 503316480 | bytes 16000000 | tf_op jit(solution)/shard_map/pallas_call | solution.py:250
  331.4 7.1 %collective-permute-start.49 = (bf16[2,32,2560]{2,1,0:T(8,128)(2,1)}, bf16[2,32,2560]{2,1,0:T(8,128)(2,1)}, u32[]{:S(2)}, u32[]{:S(2)}) collective-permute-start(bf16[2,32,2560]{2,1,0:T(8,128)(2,1)} %shard_map.97), channel_id=1, source_target_pairs={{0,63},{1,32},{2,33},{3,34},{4,35},{5,36},{6,37},{7,38},{8,39},{9,... | collective-permute-start | bytes 983048 | tf_op jit(solution)/shard_map/ppermute | solution.py:333
  341.4 6.5 %shard_map.98 = (bf16[2,32,2560]{2,1,0:T(8,128)(2,1)}, bf16[2,32,5120]{2,1,0:T(8,128)(2,1)}, f32[2,32,2560]{2,1,0:T(8,128)}, f32[2,64,128]{2,1,0:T(8,128)}, f32[...) custom-call(s32[3]{0:T(128)} %add_add_fusion.5.where_ref, ...), custom_call_target="tpu_custom_call", output_to_operand_aliasing={{5}: (15, {})} | custom-call | flops 503316480 | bytes 16000000 | tf_op jit(solution)/shard_map/pallas_call | solution.py:250
  380.2 6.5 %shard_map.100 = (bf16[2,32,2560]{2,1,0:T(8,128)(2,1)}, bf16[2,32,5120]{2,1,0:T(8,128)(2,1)}, f32[2,32,2560]{2,1,0:T(8,128)}, f32[2,64,128]{2,1,0:T(8,128)}, f32...) custom-call(s32[3]{0:T(128)} %add_add_fusion.4.where_ref, ...), custom_call_target="tpu_custom_call", output_to_operand_aliasing={{5}: (15, {})} | custom-call | flops 503316480 | bytes 16000000 | tf_op jit(solution)/shard_map/pallas_call | solution.py:250
  396.3 7.2 %collective-permute-done.57.self_ref.refs_0_ = bf16[2,32,2560]{2,1,0:T(8,128)(2,1)S(1)} collective-permute-done((bf16[2,32,2560]{2,1,0:T(8,128)(2,1)}, bf16[2,32,2560]{2,1,0:T(8,128)(2,1)S(1)}, u32[]{:S(2)}, u32[]{:S(2)}) %collective-permute-start.57) | collective-permute-done | bytes 327712 | tf_op jit(solution)/shard_map/ppermute | solution.py:333
  404.2 6.4 %shard_map.102 = (bf16[2,32,2560]{2,1,0:T(8,128)(2,1)}, bf16[2,32,5120]{2,1,0:T(8,128)(2,1)}, f32[2,32,2560]{2,1,0:T(8,128)}, f32[2,64,128]{2,1,0:T(8,128)}, f32...) custom-call(s32[3]{0:T(128)} %add_add_fusion.3.where_ref, ...), custom_call_target="tpu_custom_call", output_to_operand_aliasing={{5}: (15, {})} | custom-call | flops 503316480 | bytes 16000000 | tf_op jit(solution)/shard_map/pallas_call | solution.py:250
  427.5 6.5 %shard_map.104 = (bf16[2,32,2560]{2,1,0:T(8,128)(2,1)}, bf16[2,32,5120]{2,1,0:T(8,128)(2,1)}, f32[2,32,2560]{2,1,0:T(8,128)}, f32[2,64,128]{2,1,0:T(8,128)}, f32...) custom-call(s32[3]{0:T(128)} %add_add_fusion.2.where_ref, ...), custom_call_target="tpu_custom_call", output_to_operand_aliasing={{5}: (15, {})} | custom-call | flops 503316480 | bytes 16000000 | tf_op jit(solution)/shard_map/pallas_call | solution.py:250
  451.0 6.6 %shard_map.106 = (bf16[2,32,2560]{2,1,0:T(8,128)(2,1)}, bf16[2,32,5120]{2,1,0:T(8,128)(2,1)}, f32[2,32,2560]{2,1,0:T(8,128)}, f32[2,64,128]{2,1,0:T(8,128)}, f32...) custom-call(s32[3]{0:T(128)} %add_add_fusion.1.where_ref, ...), custom_call_target="tpu_custom_call", output_to_operand_aliasing={{5}: (15, {})} | custom-call | flops 503316480 | bytes 16000000 | tf_op jit(solution)/shard_map/pallas_call | solution.py:250
  473.6 7.7 %collective-permute-start.78 = (bf16[2,32,2560]{2,1,0:T(8,128)(2,1)S(1)}, bf16[2,32,2560]{2,1,0:T(8,128)(2,1)S(1)}, u32[]{:S(2)}, u32[]{:S(2)}) collective-permute-start(bf16[2,32,2560]{2,1,0:T(8,128)(2,1)S(1)} %copy-done.55), channel_id=1, source_target_pairs={{0,0},{32,32},{64,64},{128,128},{160,160},{192,192},{224,96},{96,2... | collective-permute-start | bytes 983048 | tf_op jit(solution)/shard_map/ppermute | solution.py:338
  483.3 7.2 %collective-permute-start.76 = (bf16[2,32,2560]{2,1,0:T(8,128)(2,1)}, bf16[2,32,2560]{2,1,0:T(8,128)(2,1)}, u32[]{:S(2)}, u32[]{:S(2)}) collective-permute-start(bf16[2,32,2560]{2,1,0:T(8,128)(2,1)} %shard_map.105), channel_id=1, source_target_pairs={{0,0},{32,32},{64,64},{96,96},{128,128},{192,192},{224,160},{160,2... | collective-permute-start | bytes 983048 | tf_op jit(solution)/shard_map/ppermute | solution.py:338
  496.1 6.7 %shard_map.108 = (bf16[2,32,2560]{2,1,0:T(8,128)(2,1)}, bf16[2,32,5120]{2,1,0:T(8,128)(2,1)}, f32[2,32,2560]{2,1,0:T(8,128)}, f32[2,64,128]{2,1,0:T(8,128)}, f32...) custom-call(s32[3]{0:T(128)} %add_add_fusion.where_ref, ...), custom_call_target="tpu_custom_call", output_to_operand_aliasing={{5}: (15, {})} | custom-call | flops 503316480 | bytes 16000000 | tf_op jit(solution)/shard_map/pallas_call | solution.py:250
  (350 shorter events, 329.1 us)
Async XLA Ops:
  33.9 40.4 %collective-permute-start.10 = (bf16[2,32,5120]{2,1,0:T(8,128)(2,1)}, bf16[2,32,5120]{2,1,0:T(8,128)(2,1)S(1)}, u32[]{:S(2)}, u32[]{:S(2)}) collective-permute-start(bf16[2,32,5120]{2,1,0:T(8,128)(2,1)} %get-tuple-element.221), channel_id=1, source_target_pairs={{0,1},{1,2},{2,3},{3,4},{4,5},{5,6},{6,7},{7,8},{8,9},{9,10},{10,1... | collective-permute-start | bytes 1966088 | tf_op jit(solution)/shard_map/ppermute | solution.py:333
  35.1 39.2 %collective-permute-start.11 = (bf16[2,32,5120]{2,1,0:T(8,128)(2,1)}, bf16[2,32,5120]{2,1,0:T(8,128)(2,1)}, u32[]{:S(2)}, u32[]{:S(2)}) collective-permute-start(bf16[2,32,5120]{2,1,0:T(8,128)(2,1)} %get-tuple-element.221), channel_id=1, source_target_pairs={{0,31},{1,0},{2,1},{3,2},{4,3},{5,4},{6,5},{7,6},{8,7},{9,8},{10,9... | collective-permute-start | bytes 1966088 | tf_op jit(solution)/shard_map/ppermute | solution.py:333
  47.9 60.6 %collective-permute-start.15 = (bf16[2,32,5120]{2,1,0:T(8,128)(2,1)}, bf16[2,32,5120]{2,1,0:T(8,128)(2,1)S(1)}, u32[]{:S(2)}, u32[]{:S(2)}) collective-permute-start(bf16[2,32,5120]{2,1,0:T(8,128)(2,1)} %get-tuple-element.220), channel_id=1, source_target_pairs={{0,1},{1,2},{2,3},{3,4},{4,5},{5,6},{6,7},{7,8},{8,9},{9,10},{10,1... | collective-permute-start | bytes 1966088 | tf_op jit(solution)/shard_map/ppermute | solution.py:333
  48.1 60.3 %collective-permute-start.16 = (bf16[2,32,5120]{2,1,0:T(8,128)(2,1)}, bf16[2,32,5120]{2,1,0:T(8,128)(2,1)S(1)}, u32[]{:S(2)}, u32[]{:S(2)}) collective-permute-start(bf16[2,32,5120]{2,1,0:T(8,128)(2,1)} %get-tuple-element.220), channel_id=1, source_target_pairs={{0,31},{1,0},{2,1},{3,2},{4,3},{5,4},{6,5},{7,6},{8,7},{9,8},{10,9... | collective-permute-start | bytes 1966088 | tf_op jit(solution)/shard_map/ppermute | solution.py:333
  103.2 35.0 %collective-permute-start.20 = (bf16[2,32,5120]{2,1,0:T(8,128)(2,1)}, bf16[2,32,5120]{2,1,0:T(8,128)(2,1)S(1)}, u32[]{:S(2)}, u32[]{:S(2)}) collective-permute-start(bf16[2,32,5120]{2,1,0:T(8,128)(2,1)} %get-tuple-element.219), channel_id=1, source_target_pairs={{0,1},{1,2},{2,3},{3,4},{4,5},{5,6},{6,7},{7,8},{8,9},{9,10},{10,1... | collective-permute-start | bytes 1966088 | tf_op jit(solution)/shard_map/ppermute | solution.py:333
  103.2 35.0 %collective-permute-start.21 = (bf16[2,32,5120]{2,1,0:T(8,128)(2,1)}, bf16[2,32,5120]{2,1,0:T(8,128)(2,1)S(1)}, u32[]{:S(2)}, u32[]{:S(2)}) collective-permute-start(bf16[2,32,5120]{2,1,0:T(8,128)(2,1)} %get-tuple-element.219), channel_id=1, source_target_pairs={{0,31},{1,0},{2,1},{3,2},{4,3},{5,4},{6,5},{7,6},{8,7},{9,8},{10,9... | collective-permute-start | bytes 1966088 | tf_op jit(solution)/shard_map/ppermute | solution.py:333
  114.4 54.4 %collective-permute-start.25 = (bf16[2,32,5120]{2,1,0:T(8,128)(2,1)}, bf16[2,32,5120]{2,1,0:T(8,128)(2,1)S(1)}, u32[]{:S(2)}, u32[]{:S(2)}) collective-permute-start(bf16[2,32,5120]{2,1,0:T(8,128)(2,1)} %get-tuple-element.218), channel_id=1, source_target_pairs={{0,1},{1,2},{2,3},{3,4},{4,5},{5,6},{6,7},{7,8},{8,9},{9,10},{10,1... | collective-permute-start | bytes 1966088 | tf_op jit(solution)/shard_map/ppermute | solution.py:333
  134.7 35.3 %collective-permute-start.26 = (bf16[2,32,5120]{2,1,0:T(8,128)(2,1)}, bf16[2,32,5120]{2,1,0:T(8,128)(2,1)S(1)}, u32[]{:S(2)}, u32[]{:S(2)}) collective-permute-start(bf16[2,32,5120]{2,1,0:T(8,128)(2,1)} %get-tuple-element.218), channel_id=1, source_target_pairs={{0,31},{1,0},{2,1},{3,2},{4,3},{5,4},{6,5},{7,6},{8,7},{9,8},{10,9... | collective-permute-start | bytes 1966088 | tf_op jit(solution)/shard_map/ppermute | solution.py:333
  143.1 58.6 %collective-permute-start.30 = (bf16[2,32,5120]{2,1,0:T(8,128)(2,1)}, bf16[2,32,5120]{2,1,0:T(8,128)(2,1)S(1)}, u32[]{:S(2)}, u32[]{:S(2)}) collective-permute-start(bf16[2,32,5120]{2,1,0:T(8,128)(2,1)} %get-tuple-element.217), channel_id=1, source_target_pairs={{0,1},{1,2},{2,3},{3,4},{4,5},{5,6},{6,7},{7,8},{8,9},{9,10},{10,1... | collective-permute-start | bytes 1966088 | tf_op jit(solution)/shard_map/ppermute | solution.py:333
  177.2 57.7 %collective-permute-start.35 = (bf16[2,32,5120]{2,1,0:T(8,128)(2,1)}, bf16[2,32,5120]{2,1,0:T(8,128)(2,1)S(1)}, u32[]{:S(2)}, u32[]{:S(2)}) collective-permute-start(bf16[2,32,5120]{2,1,0:T(8,128)(2,1)} %get-tuple-element.216), channel_id=1, source_target_pairs={{0,1},{1,2},{2,3},{3,4},{4,5},{5,6},{6,7},{7,8},{8,9},{9,10},{10,1... | collective-permute-start | bytes 1966088 | tf_op jit(solution)/shard_map/ppermute | solution.py:333
  178.6 56.3 %collective-permute-start.36 = (bf16[2,32,5120]{2,1,0:T(8,128)(2,1)}, bf16[2,32,5120]{2,1,0:T(8,128)(2,1)S(1)}, u32[]{:S(2)}, u32[]{:S(2)}) collective-permute-start(bf16[2,32,5120]{2,1,0:T(8,128)(2,1)} %get-tuple-element.216), channel_id=1, source_target_pairs={{0,31},{1,0},{2,1},{3,2},{4,3},{5,4},{6,5},{7,6},{8,7},{9,8},{10,9... | collective-permute-start | bytes 1966088 | tf_op jit(solution)/shard_map/ppermute | solution.py:333
  213.0 56.0 %collective-permute-start.40 = (bf16[2,32,5120]{2,1,0:T(8,128)(2,1)}, bf16[2,32,5120]{2,1,0:T(8,128)(2,1)S(1)}, u32[]{:S(2)}, u32[]{:S(2)}) collective-permute-start(bf16[2,32,5120]{2,1,0:T(8,128)(2,1)} %get-tuple-element.215), channel_id=1, source_target_pairs={{0,1},{1,2},{2,3},{3,4},{4,5},{5,6},{6,7},{7,8},{8,9},{9,10},{10,1... | collective-permute-start | bytes 1966088 | tf_op jit(solution)/shard_map/ppermute | solution.py:333
  213.8 55.3 %collective-permute-start.41 = (bf16[2,32,5120]{2,1,0:T(8,128)(2,1)}, bf16[2,32,5120]{2,1,0:T(8,128)(2,1)S(1)}, u32[]{:S(2)}, u32[]{:S(2)}) collective-permute-start(bf16[2,32,5120]{2,1,0:T(8,128)(2,1)} %get-tuple-element.215), channel_id=1, source_target_pairs={{0,31},{1,0},{2,1},{3,2},{4,3},{5,4},{6,5},{7,6},{8,7},{9,8},{10,9... | collective-permute-start | bytes 1966088 | tf_op jit(solution)/shard_map/ppermute | solution.py:333
  263.3 36.2 %collective-permute-start.45 = (bf16[2,32,5120]{2,1,0:T(8,128)(2,1)}, bf16[2,32,5120]{2,1,0:T(8,128)(2,1)S(1)}, u32[]{:S(2)}, u32[]{:S(2)}) collective-permute-start(bf16[2,32,5120]{2,1,0:T(8,128)(2,1)} %get-tuple-element.214), channel_id=1, source_target_pairs={{0,1},{1,2},{2,3},{3,4},{4,5},{5,6},{6,7},{7,8},{8,9},{9,10},{10,1... | collective-permute-start | bytes 1966088 | tf_op jit(solution)/shard_map/ppermute | solution.py:333
  263.3 36.5 %collective-permute-start.46 = (bf16[2,32,5120]{2,1,0:T(8,128)(2,1)}, bf16[2,32,5120]{2,1,0:T(8,128)(2,1)S(1)}, u32[]{:S(2)}, u32[]{:S(2)}) collective-permute-start(bf16[2,32,5120]{2,1,0:T(8,128)(2,1)} %get-tuple-element.214), channel_id=1, source_target_pairs={{0,31},{1,0},{2,1},{3,2},{4,3},{5,4},{6,5},{7,6},{8,7},{9,8},{10,9... | collective-permute-start | bytes 1966088 | tf_op jit(solution)/shard_map/ppermute | solution.py:333
  274.2 54.0 %collective-permute-start.50 = (bf16[2,32,5120]{2,1,0:T(8,128)(2,1)}, bf16[2,32,5120]{2,1,0:T(8,128)(2,1)S(1)}, u32[]{:S(2)}, u32[]{:S(2)}) collective-permute-start(bf16[2,32,5120]{2,1,0:T(8,128)(2,1)} %get-tuple-element.213), channel_id=1, source_target_pairs={{0,1},{1,2},{2,3},{3,4},{4,5},{5,6},{6,7},{7,8},{8,9},{9,10},{10,1... | collective-permute-start | bytes 1966088 | tf_op jit(solution)/shard_map/ppermute | solution.py:333
  296.6 34.8 %collective-permute-start.51 = (bf16[2,32,5120]{2,1,0:T(8,128)(2,1)}, bf16[2,32,5120]{2,1,0:T(8,128)(2,1)S(1)}, u32[]{:S(2)}, u32[]{:S(2)}) collective-permute-start(bf16[2,32,5120]{2,1,0:T(8,128)(2,1)} %get-tuple-element.213), channel_id=1, source_target_pairs={{0,31},{1,0},{2,1},{3,2},{4,3},{5,4},{6,5},{7,6},{8,7},{9,8},{10,9... | collective-permute-start | bytes 1966088 | tf_op jit(solution)/shard_map/ppermute | solution.py:333
  305.2 54.0 %collective-permute-start.55 = (bf16[2,32,5120]{2,1,0:T(8,128)(2,1)}, bf16[2,32,5120]{2,1,0:T(8,128)(2,1)S(1)}, u32[]{:S(2)}, u32[]{:S(2)}) collective-permute-start(bf16[2,32,5120]{2,1,0:T(8,128)(2,1)} %get-tuple-element.212), channel_id=1, source_target_pairs={{0,1},{1,2},{2,3},{3,4},{4,5},{5,6},{6,7},{7,8},{8,9},{9,10},{10,1... | collective-permute-start | bytes 1966088 | tf_op jit(solution)/shard_map/ppermute | solution.py:333
  339.3 53.9 %collective-permute-start.60 = (bf16[2,32,5120]{2,1,0:T(8,128)(2,1)}, bf16[2,32,5120]{2,1,0:T(8,128)(2,1)S(1)}, u32[]{:S(2)}, u32[]{:S(2)}) collective-permute-start(bf16[2,32,5120]{2,1,0:T(8,128)(2,1)} %get-tuple-element.211), channel_id=1, source_target_pairs={{0,1},{1,2},{2,3},{3,4},{4,5},{5,6},{6,7},{7,8},{8,9},{9,10},{10,1... | collective-permute-start | bytes 1966088 | tf_op jit(solution)/shard_map/ppermute | solution.py:333
  339.3 54.0 %collective-permute-start.61 = (bf16[2,32,5120]{2,1,0:T(8,128)(2,1)}, bf16[2,32,5120]{2,1,0:T(8,128)(2,1)}, u32[]{:S(2)}, u32[]{:S(2)}) collective-permute-start(bf16[2,32,5120]{2,1,0:T(8,128)(2,1)} %get-tuple-element.211), channel_id=1, source_target_pairs={{0,31},{1,0},{2,1},{3,2},{4,3},{5,4},{6,5},{7,6},{8,7},{9,8},{10,9... | collective-permute-start | bytes 1966088 | tf_op jit(solution)/shard_map/ppermute | solution.py:333
  365.0 55.4 %collective-permute-start.65 = (bf16[2,32,5120]{2,1,0:T(8,128)(2,1)}, bf16[2,32,5120]{2,1,0:T(8,128)(2,1)S(1)}, u32[]{:S(2)}, u32[]{:S(2)}) collective-permute-start(bf16[2,32,5120]{2,1,0:T(8,128)(2,1)} %get-tuple-element.224), channel_id=1, source_target_pairs={{0,1},{1,2},{2,3},{3,4},{4,5},{5,6},{6,7},{7,8},{8,9},{9,10},{10,1... | collective-permute-start | bytes 1966088 | tf_op jit(solution)/shard_map/ppermute | solution.py:333
  373.9 46.7 %collective-permute-start.66 = (bf16[2,32,5120]{2,1,0:T(8,128)(2,1)}, bf16[2,32,5120]{2,1,0:T(8,128)(2,1)S(1)}, u32[]{:S(2)}, u32[]{:S(2)}) collective-permute-start(bf16[2,32,5120]{2,1,0:T(8,128)(2,1)} %get-tuple-element.224), channel_id=1, source_target_pairs={{0,31},{1,0},{2,1},{3,2},{4,3},{5,4},{6,5},{7,6},{8,7},{9,8},{10,9... | collective-permute-start | bytes 1966088 | tf_op jit(solution)/shard_map/ppermute | solution.py:333
  469.5 39.2 %collective-permute-start.79 = (bf16[2,32,2560]{2,1,0:T(8,128)(2,1)S(1)}, bf16[2,32,2560]{2,1,0:T(8,128)(2,1)S(1)}, u32[]{:S(2)}, u32[]{:S(2)}) collective-permute-start(bf16[2,32,2560]{2,1,0:T(8,128)(2,1)S(1)} %copy-done.54), channel_id=1, source_target_pairs={{0,0},{32,32},{96,96},{128,128},{160,160},{192,192},{224,64},{64,2... | collective-permute-start | bytes 983048 | tf_op jit(solution)/shard_map/ppermute | solution.py:338
  473.6 35.1 %collective-permute-start.78 = (bf16[2,32,2560]{2,1,0:T(8,128)(2,1)S(1)}, bf16[2,32,2560]{2,1,0:T(8,128)(2,1)S(1)}, u32[]{:S(2)}, u32[]{:S(2)}) collective-permute-start(bf16[2,32,2560]{2,1,0:T(8,128)(2,1)S(1)} %copy-done.55), channel_id=1, source_target_pairs={{0,0},{32,32},{64,64},{128,128},{160,160},{192,192},{224,96},{96,2... | collective-permute-start | bytes 983048 | tf_op jit(solution)/shard_map/ppermute | solution.py:338
  (123 other events, 1637.6 us)
